TPU v7x, 32 devices: a whole 2x2x4 slice. The times are simulated.
32 devices in a mesh: groups: 2 (over x), side: 16 (over z, y, core).
Axes of the slice: x: 2, y: 2, z: 4, core: 2. Of those that a mesh axis runs over, the one named last changes fastest.
Arguments:
- query: bfloat16 [256, 3072], P(('groups', 'side')), parts along dimension 0, may hold values from -48 to 48
- new_key: bfloat16 [256, 512], P(('groups', 'side')), parts along dimension 0, may hold values from -6 to 6
- new_value: bfloat16 [256, 512], P(('groups', 'side')), parts along dimension 0, may hold values from -6 to 6
- key_cache: bfloat16 [256, 128, 512], P(('groups', 'side')), parts along dimension 0, may hold values from -6 to 6
- value_cache: bfloat16 [256, 128, 512], P(('groups', 'side')), parts along dimension 0, may hold values from -6 to 6
- lengths: int32 [256], P(('groups', 'side')), parts along dimension 0, may hold values from 2 to 128
- residual: bfloat16 [256, 3072], P(('groups', 'side')), parts along dimension 0, may hold values from -6 to 6
- norm_gain: bfloat16 [3072], replicated, may hold values from 0.3984375 to 1.59375
- router: bfloat16 [3072, 8], replicated, may hold values from -0.109375 to 0.109375
- routes: int32 [256, 2], P(('groups', 'side')), parts along dimension 0, may hold values from 0 to 7, all different within a row; in each aligned block of 4 rows (0 to 3, 4 to 7, ...) at most 2 rows name the same one
- w_gate: bfloat16 [3072, 8192], P(None, 'side'), may hold values from -0.109375 to 0.109375
- w_up: bfloat16 [3072, 8192], P(None, 'side'), may hold values from -0.109375 to 0.109375
- w_down: bfloat16 [8192, 3072], P('side'), may hold values from -0.1875 to 0.1875
Outputs:
- layer_output: bfloat16 [256, 3072], P(('groups', 'side')), parts along dimension 0
There are 2 independent parts, one for each index of `groups`. A program takes and returns all parts, laid end to end along the dimension named above; an argument that names none is the same for every part. Nothing has to cross between parts.
Inputs may be any that keep to these rules, and one draw needn't show every extreme that they name: `routes`: in each aligned block of 4 sequences (each half of one device's sequences) no expert is named by more than 2 of them.
All inputs are finite; a program needn't handle non-finite values.
Results may differ from a plain program's by a relative error of at most 0.0065.
Values may be sent and summed in bfloat16 or wider, within the bound.
A program may use at most 128 MiB of HBM per device.

v0:
```python
import jax
import jax.numpy as jnp
from jax import lax
from jax.sharding import PartitionSpec as P

HD = 128


def attend(query, new_key, new_value, key_cache, value_cache, lengths):
    seq_count = query.shape[0]
    head_size = HD
    kv_heads = new_key.shape[1] // head_size
    group = query.shape[1] // new_key.shape[1]
    slots = key_cache.shape[1]
    scale = head_size ** (-0.5)
    q_heads = query.reshape(seq_count, kv_heads, group, head_size)
    keys = key_cache.reshape(seq_count, slots, kv_heads, head_size)
    values = value_cache.reshape(seq_count, slots, kv_heads, head_size)
    own_key = new_key.reshape(seq_count, kv_heads, head_size)
    own_value = new_value.reshape(seq_count, kv_heads, head_size)
    scores = (
        jnp.einsum("sjgd,sljd->sjgl", q_heads, keys, preferred_element_type=jnp.float32) * scale
    )
    own_score = (
        jnp.einsum("sjgd,sjd->sjg", q_heads, own_key, preferred_element_type=jnp.float32) * scale
    )
    live = jnp.arange(slots, dtype=jnp.int32)[None, :] < lengths[:, None]
    scores = jnp.where(live[:, None, None, :], scores, -jnp.inf)
    top_score = jnp.maximum(jnp.max(scores, axis=-1), own_score)
    weights = jnp.exp(scores - top_score[..., None])
    own_weight = jnp.exp(own_score - top_score)
    total = jnp.sum(weights, axis=-1) + own_weight
    mixed = jnp.einsum(
        "sjgl,sljd->sjgd", weights.astype(jnp.bfloat16), values, preferred_element_type=jnp.float32
    )
    mixed = (
        mixed
        + own_weight.astype(jnp.bfloat16).astype(jnp.float32)[..., None]
        * own_value.astype(jnp.float32)[:, :, None, :]
    )
    return (mixed / total[..., None]).reshape(seq_count, kv_heads * group * head_size)


def expert_rows(tok_rows, w_gate, w_up, w_down):
    gate_part = jnp.dot(tok_rows, w_gate, preferred_element_type=jnp.float32)
    up_part = jnp.dot(tok_rows, w_up, preferred_element_type=jnp.float32)
    hidden = (jax.nn.silu(gate_part) * up_part).astype(jnp.bfloat16)
    return jnp.dot(hidden, w_down, preferred_element_type=jnp.float32)


def on_device(
    query,
    new_key,
    new_value,
    key_cache,
    value_cache,
    lengths,
    residual,
    norm_gain,
    router,
    routes,
    w_gate,
    w_up,
    w_down,
):
    seq_count = query.shape[0]
    experts_all = router.shape[1]
    width = residual.shape[1]
    side_count = lax.axis_size("side")
    group_size = side_count // experts_all
    batch_rows = seq_count // 2
    capacity = batch_rows // 2
    expert_ids = jnp.arange(experts_all, dtype=jnp.int32)
    slot_ids = jnp.arange(capacity, dtype=jnp.int32).astype(jnp.float32)
    positions = jnp.arange(batch_rows, dtype=jnp.int32)
    earlier = (positions[:, None] > positions[None, :]).astype(jnp.float32)
    results = []
    for index_half in range(2):
        lower = index_half * batch_rows
        upper = lower + batch_rows
        attention = attend(
            query[lower:upper],
            new_key[lower:upper],
            new_value[lower:upper],
            key_cache[lower:upper],
            value_cache[lower:upper],
            lengths[lower:upper],
        )
        mid_f = (
            (residual[lower:upper].astype(jnp.float32) + attention)
            .astype(jnp.bfloat16)
            .astype(jnp.float32)
        )
        normed = (
            mid_f
            * lax.rsqrt(jnp.mean(mid_f * mid_f, axis=-1, keepdims=True) + 1e-05)
            * norm_gain.astype(jnp.float32)
        ).astype(jnp.bfloat16)
        logits = jnp.dot(normed, router, preferred_element_type=jnp.float32)
        onehot = (routes[lower:upper, :, None] == expert_ids[None, None, :]).astype(jnp.float32)
        chosen = jnp.sum(onehot * logits[:, None, :], axis=-1)
        first = jax.nn.sigmoid(chosen[:, 0] - chosen[:, 1])
        second = jax.nn.sigmoid(chosen[:, 1] - chosen[:, 0])
        gates = (first[:, None] * onehot[:, 0] + second[:, None] * onehot[:, 1]).astype(
            jnp.bfloat16
        )
        routed = jnp.sum(onehot, axis=1)
        rank = jnp.dot(earlier, routed, precision=lax.Precision.HIGHEST)
        select = routed.T[:, None, :] * (rank.T[:, None, :] == slot_ids[None, :, None]).astype(
            jnp.float32
        )
        packed = jnp.einsum(
            "ect,td->ecd", select.astype(jnp.bfloat16), normed, preferred_element_type=jnp.float32
        ).astype(jnp.bfloat16)
        outgoing = jnp.broadcast_to(
            packed[:, None], (experts_all, group_size, capacity, width)
        ).reshape(side_count, capacity, width)
        arrived = lax.all_to_all(outgoing, "side", split_axis=0, concat_axis=0, tiled=True)
        sources = arrived.shape[0]
        items = arrived.shape[1]
        partial_value = expert_rows(arrived.reshape(sources * items, width), w_gate, w_up, w_down)
        returned = lax.all_to_all(
            partial_value.reshape(sources, items, width).astype(jnp.bfloat16),
            "side",
            split_axis=0,
            concat_axis=0,
            tiled=True,
        ).astype(jnp.float32)
        summed = jnp.sum(returned.reshape(experts_all, group_size, capacity, width), axis=1)
        weighted = select * gates.astype(jnp.float32).T[:, None, :]
        moe = jnp.einsum("ect,ecd->td", weighted, summed, precision=lax.Precision.HIGHEST)
        results.append((mid_f + moe).astype(jnp.bfloat16))
    return jnp.concatenate(results, axis=0)


def solution(mesh):
    in_specs = (
        P(("groups", "side"), None),
        P(("groups", "side"), None),
        P(("groups", "side"), None),
        P(("groups", "side"), None, None),
        P(("groups", "side"), None, None),
        P(("groups", "side")),
        P(("groups", "side"), None),
        P(),
        P(),
        P(("groups", "side"), None),
        P(None, "side"),
        P(None, "side"),
        P("side", None),
    )
    out_specs = P(("groups", "side"), None)
    return jax.shard_map(
        on_device, mesh=mesh, in_specs=in_specs, out_specs=out_specs, check_vma=False
    )
```

profile of v0, /device:TPU:0, one launch (start us, length us, event | category | flops | bytes accessed | tf_op | source)
XLA Modules:
  0.0 86.5 jit_solution(12987751732217031285)
XLA Ops:
  5.0 2.3 %fusion.86 = (bf16[4,128,512]{2,1,0:T(8,128)(2,1)}, bf16[4,128,512]{2,1,0:T(8,128)(2,1)}) fusion(bf16[8,128,512]{2,1,0:T(8,128)(2,1)} %param.16), kind=kLoop, calls=%fused_computation.135 | loop fusion | bytes 2097152 | tf_op jit(solution)/shard_map/slice | solution.py:85
  7.3 2.1 %copy.46 = bf16[4,128,512]{1,2,0:T(8,128)(2,1)} copy(bf16[4,128,512]{2,1,0:T(8,128)(2,1)} %get-tuple-element.13) | data formatting | bytes 1048576
  9.6 1.4 %fusion.92 = (f32[4,4,6]{2,1,0:T(4,128)S(1)}, f32[4,4,6,128]{3,2,1,0:T(8,128)S(1)}) fusion(bf16[4,4,6,128]{3,2,1,0:T(8,128)(2,1)S(1)} %reshape.147, bf16[4,128,4,128]{1,3,2,0:T(8,128)(2,1)} %bitcast.108, pred[4,128]{1,0:T(4,128)(4,1)S(1)} %get-tuple-element.42), kind=kOutput, calls=%fused_computation.141 | convolution fusion | flops 3182496 | bytes 598912 | tf_op jit(solution)/shard_map/sjgd,sljd->sjgl/dot_general | solution.py:22
  11.2 2.1 %copy.48 = bf16[4,128,512]{1,2,0:T(8,128)(2,1)} copy(bf16[4,128,512]{2,1,0:T(8,128)(2,1)} %get-tuple-element.14) | data formatting | bytes 1048576
  13.4 1.4 %fusion.93 = (f32[4,4,6]{2,1,0:T(4,128)S(1)}, f32[4,4,6,128]{3,2,1,0:T(8,128)S(1)}) fusion(bf16[4,4,6,128]{3,2,1,0:T(8,128)(2,1)S(1)} %reshape.156, bf16[4,128,4,128]{1,3,2,0:T(8,128)(2,1)} %bitcast.109, pred[4,128]{1,0:T(4,128)(4,1)S(1)} %get-tuple-element.41), kind=kOutput, calls=%fused_computation.142 | convolution fusion | flops 3182496 | bytes 598912 | tf_op jit(solution)/shard_map/sjgd,sljd->sjgl/dot_general | solution.py:22
  15.0 2.3 %fusion.87 = (bf16[4,128,512]{2,1,0:T(8,128)(2,1)}, bf16[4,128,512]{2,1,0:T(8,128)(2,1)}) fusion(bf16[8,128,512]{2,1,0:T(8,128)(2,1)} %param.17), kind=kLoop, calls=%fused_computation.136 | loop fusion | bytes 2097152 | tf_op jit(solution)/shard_map/slice | solution.py:86
  17.2 2.1 %copy.47 = bf16[4,128,512]{1,2,0:T(8,128)(2,1)} copy(bf16[4,128,512]{2,1,0:T(8,128)(2,1)} %get-tuple-element.15) | data formatting | bytes 1048576
  19.3 1.5 %fusion.5 = f32[4,4,6,128]{3,2,1,0:T(8,128)S(1)} fusion(bf16[4,128,4,128]{1,3,2,0:T(8,128)(2,1)} %bitcast.110, f32[4,4,6,128]{3,2,1,0:T(8,128)S(1)} %get-tuple-element.38, f32[4,4,6]{2,1,0:T(4,128)S(1)} %get-tuple-element.22, f32[4,4,128]{2,1,0:T(4,128)S(1)} %reshape.165, f32[4,4,6]{2,1,0:T(4,128)S(1)} %get-tuple-element.21, ...), kind=kOutput, calls=%fused_computation.17 | convolution fusion | flops 3207168 | bytes 631936 | tf_op jit(solution)/shard_map/sjgl,sljd->sjgd/dot_general | solution.py:33
  20.8 2.1 %copy.49 = bf16[4,128,512]{1,2,0:T(8,128)(2,1)} copy(bf16[4,128,512]{2,1,0:T(8,128)(2,1)} %get-tuple-element.16) | data formatting | bytes 1048576
  22.9 1.5 %fusion.7 = f32[4,4,6,128]{3,2,1,0:T(8,128)S(1)} fusion(bf16[4,128,4,128]{1,3,2,0:T(8,128)(2,1)} %bitcast.111, f32[4,4,6,128]{3,2,1,0:T(8,128)S(1)} %get-tuple-element.40, f32[4,4,6]{2,1,0:T(4,128)S(1)} %get-tuple-element.24, f32[4,4,128]{2,1,0:T(4,128)S(1)} %reshape.168, f32[4,4,6]{2,1,0:T(4,128)S(1)} %get-tuple-element.23, ...), kind=kOutput, calls=%fused_computation.19 | convolution fusion | flops 3207168 | bytes 631936 | tf_op jit(solution)/shard_map/sjgl,sljd->sjgd/dot_general | solution.py:33
  27.0 7.4 %all-to-all-start.2 = ((bf16[16,2,3072]{2,1,0:T(2,128)(2,1)}), bf16[16,2,3072]{2,1,0:T(2,128)(2,1)S(1)}, u32[]{:S(2)}, u32[]{:S(2)}) async-start(bf16[16,2,3072]{2,1,0:T(2,128)(2,1)} %bitcast.25), calls=%async_computation.2 | async-start | bytes 393216 | tf_op jit(solution)/shard_map/all_to_all | solution.py:118
  38.8 4.7 %all-to-all-done.2 = bf16[16,2,3072]{2,1,0:T(2,128)(2,1)S(1)} async-done(((bf16[16,2,3072]{2,1,0:T(2,128)(2,1)}), bf16[16,2,3072]{2,1,0:T(2,128)(2,1)S(1)}, u32[]{:S(2)}, u32[]{:S(2)}) %all-to-all-start.2) | async-done | bytes 196640 | tf_op jit(solution)/shard_map/all_to_all | solution.py:118
  44.2 4.2 %all-to-all-start = ((bf16[16,2,3072]{2,1,0:T(2,128)(2,1)}), bf16[16,2,3072]{2,1,0:T(2,128)(2,1)}, u32[]{:S(2)}, u32[]{:S(2)}) async-start(bf16[16,2,3072]{2,1,0:T(2,128)(2,1)} %bitcast.11), calls=%async_computation | async-start | bytes 393216 | tf_op jit(solution)/shard_map/all_to_all | solution.py:118
  48.5 3.2 %fusion.97 = f32[32,512]{1,0:T(8,128)} fusion(bf16[32,3072]{1,0:T(8,128)(2,1)S(1)} %reshape.162, bf16[3072,512]{1,0:T(8,128)(2,1)} %param.23), kind=kOutput, calls=%fused_computation.146 | convolution fusion | flops 100663296 | bytes 3407872 | tf_op jit(solution)/shard_map/dot_general | solution.py:45
  51.6 3.1 %convolution_convert_fusion = bf16[32,3072]{1,0:T(8,128)(2,1)S(1)} fusion(bf16[512,3072]{1,0:T(8,128)(2,1)S(1)} %copy-done, bf16[32,3072]{1,0:T(8,128)(2,1)S(1)} %reshape.162, bf16[3072,512]{1,0:T(8,128)(2,1)} %param.24, f32[32,512]{1,0:T(8,128)} %fusion.97), kind=kOutput, calls=%fused_computation | convolution fusion | flops 201523200 | bytes 6750208 | tf_op jit(solution)/shard_map/dot_general | solution.py:48
  55.5 1.9 %all-to-all-done = bf16[16,2,3072]{2,1,0:T(2,128)(2,1)} async-done(((bf16[16,2,3072]{2,1,0:T(2,128)(2,1)}), bf16[16,2,3072]{2,1,0:T(2,128)(2,1)}, u32[]{:S(2)}, u32[]{:S(2)}) %all-to-all-start) | async-done | bytes 196640 | tf_op jit(solution)/shard_map/all_to_all | solution.py:118
  57.4 4.2 %all-to-all-start.3 = ((bf16[16,2,3072]{2,1,0:T(2,128)(2,1)}), bf16[16,2,3072]{2,1,0:T(2,128)(2,1)}, u32[]{:S(2)}, u32[]{:S(2)}) async-start(bf16[16,2,3072]{2,1,0:T(2,128)(2,1)} %convert_element_type.164), calls=%async_computation.3 | async-start | bytes 393216 | tf_op jit(solution)/shard_map/all_to_all | solution.py:122
  62.6 3.2 %fusion.95 = f32[32,512]{1,0:T(8,128)} fusion(bf16[32,3072]{1,0:T(8,128)(2,1)S(1)} %reshape.153, bf16[3072,512]{1,0:T(8,128)(2,1)} %param.23), kind=kOutput, calls=%fused_computation.144 | convolution fusion | flops 100663296 | bytes 3407872 | tf_op jit(solution)/shard_map/dot_general | solution.py:45
  65.7 3.1 %convolution_convert_fusion.1 = bf16[32,3072]{1,0:T(8,128)(2,1)S(1)} fusion(bf16[512,3072]{1,0:T(8,128)(2,1)S(1)} %copy-done, bf16[32,3072]{1,0:T(8,128)(2,1)S(1)} %reshape.153, bf16[3072,512]{1,0:T(8,128)(2,1)} %param.24, f32[32,512]{1,0:T(8,128)} %fusion.95), kind=kOutput, calls=%fused_computation.1 | convolution fusion | flops 201523200 | bytes 6750208 | tf_op jit(solution)/shard_map/dot_general | solution.py:48
  70.6 5.0 %all-to-all-start.1 = ((bf16[16,2,3072]{2,1,0:T(2,128)(2,1)}), bf16[16,2,3072]{2,1,0:T(2,128)(2,1)S(1)}, u32[]{:S(2)}, u32[]{:S(2)}) async-start(bf16[16,2,3072]{2,1,0:T(2,128)(2,1)} %convert_element_type.147), calls=%async_computation.1 | async-start | bytes 393216 | tf_op jit(solution)/shard_map/all_to_all | solution.py:122
  76.3 1.2 %convert_reduce_fusion = f32[8,2,3072]{2,1,0:T(2,128)S(1)} fusion(bf16[16,2,3072]{2,1,0:T(2,128)(2,1)} %all-to-all-done.3), kind=kLoop, calls=%fused_computation.22 | loop fusion | flops 147456 | bytes 393216 | tf_op jit(solution)/shard_map/reduce_sum | solution.py:129
  77.6 1.1 %fusion.3 = bf16[4,3072]{1,0:T(4,128)(2,1)S(1)} fusion(f32[8,2,3072]{2,1,0:T(2,128)S(1)} %convert_reduce_fusion, bf16[4,3072]{1,0:T(4,128)(2,1)} %copy-done.2, f32[8,4]{0,1:T(4,128)} %convert_bitcast_fusion, f32[8,4]{0,1:T(4,128)S(1)} %bitcast.113, f32[8,4]{0,1:T(4,128)S(1)} %fusion.64, f32[2]{0:T(128)} %copy-done.4), kind=kOutput, calls=%fused_computation.9 | convolution fusion | flops 2396352 | bytes 246152 | tf_op jit(solution)/shard_map/ect,ecd->td/dot_general | solution.py:131
  78.7 5.9 %all-to-all-done.1 = bf16[16,2,3072]{2,1,0:T(2,128)(2,1)S(1)} async-done(((bf16[16,2,3072]{2,1,0:T(2,128)(2,1)}), bf16[16,2,3072]{2,1,0:T(2,128)(2,1)S(1)}, u32[]{:S(2)}, u32[]{:S(2)}) %all-to-all-start.1) | async-done | bytes 196640 | tf_op jit(solution)/shard_map/all_to_all | solution.py:122
  84.8 1.1 %fusion.1 = bf16[4,3072]{1,0:T(4,128)(2,1)S(1)} fusion(f32[8,2,3072]{2,1,0:T(2,128)S(1)} %convert_reduce_fusion.1, bf16[4,3072]{1,0:T(4,128)(2,1)} %copy-done.1, f32[8,4]{0,1:T(4,128)S(1)} %convert_bitcast_fusion.1, f32[8,4]{0,1:T(4,128)S(1)} %bitcast.115, f32[8,4]{0,1:T(4,128)S(1)} %fusion.65, f32[2]{0:T(128)} %copy-done.4), kind=kOutput, calls=%fused_computation.7 | convolution fusion | flops 2396352 | bytes 246152 | tf_op jit(solution)/shard_map/ect,ecd->td/dot_general | solution.py:131
  (62 shorter events, 18.7 us)
Async XLA Ops:
  0.0 51.6 %copy-start = (bf16[512,3072]{1,0:T(8,128)(2,1)S(1)}, bf16[512,3072]{1,0:T(8,128)(2,1)}, u32[]{:S(2)}) copy-start(bf16[512,3072]{1,0:T(8,128)(2,1)} %param.25) | copy-start | bytes 9437188
  0.0 25.8 %copy-start.4 = (f32[2]{0:T(128)}, f32[2]{0:T(128)S(1)}, u32[]{:S(2)}) copy-start(f32[2]{0:T(128)S(1)} %iota_convert_fusion) | copy-start | bytes 28
  14.9 9.4 %copy-start.3 = (bf16[8,3072]{1,0:T(8,128)(2,1)S(1)}, bf16[8,3072]{1,0:T(8,128)(2,1)}, u32[]{:S(2)}) copy-start(bf16[8,3072]{1,0:T(8,128)(2,1)} %param.19) | copy-start | bytes 147460
  24.5 1.3 %copy-start.2 = (bf16[4,3072]{1,0:T(4,128)(2,1)}, bf16[4,3072]{1,0:T(4,128)(2,1)S(1)}, u32[]{:S(2)}) copy-start(bf16[4,3072]{1,0:T(4,128)(2,1)S(1)} %get-tuple-element.18) | copy-start | bytes 73732
  24.5 11.9 %copy-start.1 = (bf16[4,3072]{1,0:T(4,128)(2,1)}, bf16[4,3072]{1,0:T(4,128)(2,1)S(1)}, u32[]{:S(2)}) copy-start(bf16[4,3072]{1,0:T(4,128)(2,1)S(1)} %get-tuple-element.10) | copy-start | bytes 73732
  27.0 16.4 %all-to-all-start.2 = ((bf16[16,2,3072]{2,1,0:T(2,128)(2,1)}), bf16[16,2,3072]{2,1,0:T(2,128)(2,1)S(1)}, u32[]{:S(2)}, u32[]{:S(2)}) async-start(bf16[16,2,3072]{2,1,0:T(2,128)(2,1)} %bitcast.25), calls=%async_computation.2 | async-start | bytes 393216 | tf_op jit(solution)/shard_map/all_to_all | solution.py:118
  44.2 13.2 %all-to-all-start = ((bf16[16,2,3072]{2,1,0:T(2,128)(2,1)}), bf16[16,2,3072]{2,1,0:T(2,128)(2,1)}, u32[]{:S(2)}, u32[]{:S(2)}) async-start(bf16[16,2,3072]{2,1,0:T(2,128)(2,1)} %bitcast.11), calls=%async_computation | async-start | bytes 393216 | tf_op jit(solution)/shard_map/all_to_all | solution.py:118
  57.4 13.2 %all-to-all-start.3 = ((bf16[16,2,3072]{2,1,0:T(2,128)(2,1)}), bf16[16,2,3072]{2,1,0:T(2,128)(2,1)}, u32[]{:S(2)}, u32[]{:S(2)}) async-start(bf16[16,2,3072]{2,1,0:T(2,128)(2,1)} %convert_element_type.164), calls=%async_computation.3 | async-start | bytes 393216 | tf_op jit(solution)/shard_map/all_to_all | solution.py:122
  70.6 14.0 %all-to-all-start.1 = ((bf16[16,2,3072]{2,1,0:T(2,128)(2,1)}), bf16[16,2,3072]{2,1,0:T(2,128)(2,1)S(1)}, u32[]{:S(2)}, u32[]{:S(2)}) async-start(bf16[16,2,3072]{2,1,0:T(2,128)(2,1)} %convert_element_type.147), calls=%async_computation.1 | async-start | bytes 393216 | tf_op jit(solution)/shard_map/all_to_all | solution.py:122
where the time goes:
time: 88 us; the launch traced here: 86.5 us
  matrix products  24.2 us (28%)
  local copies, waits for them, and re-layouts  20.7 us (24%)
  starting transfers between devices  20.7 us (24%)
  waiting for transfers between devices  13.4 us (15%)
  other arithmetic  7.32 us (8%)
    all_to_all x2, starting transfers between devices, on_device(): lax.all_to_all(outgoing, 'side', split_axis=0, concat_axis=0, tiled=True)  11.6 us
    all_to_all x2, starting transfers between devices, on_device(): lax.all_to_all(partial_value.reshape(sources, items, width).astype(jnp.bf...  9.14 us
    unnamed x14, local copies, waits for them, and re-layouts  8.27 us
    all_to_all x2, waiting for transfers between devices, on_device(): lax.all_to_all(partial_value.reshape(sources, items, width).astype(jnp.bf...  6.83 us
    all_to_all x2, waiting for transfers between devices, on_device(): lax.all_to_all(outgoing, 'side', split_axis=0, concat_axis=0, tiled=True)  6.53 us
    dot_general x2, matrix products, expert_rows(): gate_part = jnp.dot(tok_rows, w_gate, preferred_element_type=jnp.float32)  6.3 us
    dot_general x2, matrix products, expert_rows(): return jnp.dot(hidden, w_down, preferred_element_type=jnp.float32)  6.29 us
    dot_general x2, matrix products, attend(): jnp.einsum('sjgl,sljd->sjgd', weights.astype(jnp.bfloat16), values, prefe...  2.91 us
  transfers between devices with their start and end apart: 4, of which 4 were waited for; matrix products, arithmetic and copies ran while one was open for 26% of the time, Pallas kernels for 0%

commit v1 on v0

v1 whole, which is shorter than its diff:
```python
import functools

import jax
import jax.numpy as jnp
from jax import lax
from jax.experimental import pallas as pl
from jax.experimental.pallas import tpu as pltpu
from jax.sharding import PartitionSpec as P

HD = 128
TILE = 16
F32 = jnp.float32
BF16 = jnp.bfloat16
MESH = pl.DeviceIdType.MESH


def dot(a, b):
    return jnp.dot(a, b, preferred_element_type=F32)


def iota(shape, dim):
    return lax.broadcasted_iota(jnp.int32, shape, dim)


def attend(query_ref, new_key_ref, new_value_ref, lengths_ref, keys, values, values_ready, q_rows, o_rows):
    seqs, width = query_ref.shape
    kv = new_key_ref.shape[1]
    heads = width // HD
    group = width // kv
    slots = keys.shape[1]
    scale = HD ** (-0.5)
    query = query_ref[...].astype(F32)
    for h in range(heads):
        q_rows[pl.ds(h, seqs, stride=heads), :] = query[:, h * HD : (h + 1) * HD]
    own_keys = new_key_ref[...].astype(F32)
    own_values = new_value_ref[...].astype(F32)
    mine = iota((heads, kv), 0) // group == iota((heads, kv), 1) // HD
    position = iota((heads, slots), 1)
    scores, own = [], []
    for s in range(seqs):
        q = q_rows[s * heads : (s + 1) * heads, :]
        wide = jnp.where(mine, jnp.concatenate([q] * (kv // HD), axis=1), 0.0)
        score = lax.dot_general(
            wide.astype(BF16), keys[s], (((1,), (1,)), ((), ())), preferred_element_type=F32
        )
        scores.append(jnp.where(position < lengths_ref[s], score * scale, -jnp.inf))
        own.append(jnp.sum(wide * own_keys[s : s + 1, :], axis=1, keepdims=True) * scale)
    values_ready()
    for s in range(seqs):
        top = jnp.maximum(jnp.max(scores[s], axis=1, keepdims=True), own[s])
        weights = jnp.exp(scores[s] - top)
        own_weight = jnp.exp(own[s] - top)
        total = jnp.sum(weights, axis=1, keepdims=True) + own_weight
        mixed = dot(weights.astype(BF16), values[s])
        mixed = mixed + own_weight.astype(BF16).astype(F32) * own_values[s : s + 1, :]
        mixed = jnp.where(mine, mixed, 0.0)
        summed = mixed[:, :HD]
        for j in range(1, kv // HD):
            summed = summed + mixed[:, j * HD : (j + 1) * HD]
        o_rows[s * heads : (s + 1) * heads, :] = summed / total
    return jnp.concatenate(
        [o_rows[pl.ds(h, seqs, stride=heads), :] for h in range(heads)], axis=1
    )


def kernel(
    side,
    query_ref,
    new_key_ref,
    new_value_ref,
    lengths_ref,
    residual_ref,
    gain_ref,
    router_ref,
    routes_ref,
    key_hbm,
    value_hbm,
    gate_hbm,
    up_hbm,
    down_hbm,
    out_ref,
    keys,
    values,
    w_gate,
    w_up,
    w_down,
    q_rows,
    o_rows,
    packed,
    arrived,
    hidden,
    partial,
    part_out,
    part_in,
    back_out,
    back_in,
    load_sem,
    send_sem,
    recv_sem,
    fsend_sem,
    frecv_sem,
    psend_sem,
    precv_sem,
    rsend_sem,
    rrecv_sem,
):
    seqs, width = residual_ref.shape
    experts = router_ref.shape[0]
    members = side // experts
    cap = seqs // 2
    cuts = TILE // cap
    piece = width // cuts
    rows = experts * TILE
    each = experts * cap
    me = lax.axis_index("side")
    chip = me // members
    lane = lax.rem(me, members)

    loads = []
    for n, (src, dst) in enumerate(
        (
            (key_hbm, keys),
            (value_hbm, values),
            (gate_hbm, w_gate),
            (up_hbm, w_up),
            (down_hbm, w_down),
        )
    ):
        load = pltpu.make_async_copy(src, dst, load_sem.at[n])
        load.start()
        loads.append(load)

    others = [lax.rem(chip + d, experts) for d in range(1, experts)]
    mates = [lax.rem(lane + j, members) for j in range(1, members)]
    barrier = pltpu.get_barrier_semaphore()
    for other in others:
        pl.semaphore_signal(
            barrier, inc=1, device_id={"side": other * members + lane}, device_id_type=MESH
        )
    for mate in mates:
        pl.semaphore_signal(
            barrier, inc=1, device_id={"side": chip * members + mate}, device_id_type=MESH
        )

    ids = iota((seqs, experts), 1)
    first_hot = (routes_ref[:, 0:1] == ids).astype(F32)
    second_hot = (routes_ref[:, 1:2] == ids).astype(F32)
    routed = (first_hot + second_hot).astype(BF16)
    earlier = (iota((seqs, seqs), 0) > iota((seqs, seqs), 1)).astype(BF16)
    rank = dot(earlier, routed).astype(BF16)
    spread = (iota((experts, rows), 0) == iota((experts, rows), 1) // TILE).astype(BF16)
    slot = lax.rem(iota((seqs, rows), 1), cap).astype(F32)
    chosen = jnp.where(dot(rank, spread) == slot, dot(routed, spread), 0.0)
    cut_mask = iota((cuts * seqs, rows), 0) // seqs == lax.rem(
        iota((cuts * seqs, rows), 1) // cap, cuts
    )
    select = jnp.where(cut_mask, jnp.concatenate([chosen] * cuts, axis=0), 0.0)

    loads[0].wait()
    attention = attend(
        query_ref, new_key_ref, new_value_ref, lengths_ref, keys, values, loads[1].wait, q_rows, o_rows
    )
    mid = (residual_ref[...].astype(F32) + attention).astype(BF16).astype(F32)
    normed = (
        mid
        * lax.rsqrt(jnp.mean(mid * mid, axis=1, keepdims=True) + 1e-05)
        * gain_ref[...].astype(F32)
    )
    stacked = jnp.concatenate(
        [normed[:, b * piece : (b + 1) * piece] for b in range(cuts)], axis=0
    ).astype(BF16)
    packed[...] = (
        dot(select.T.astype(BF16), stacked).astype(BF16).reshape(experts, TILE, piece)
    )

    pl.semaphore_wait(barrier, len(others) + len(mates))
    sends = []
    for d, other in enumerate(others):
        copy = pltpu.make_async_remote_copy(
            src_ref=packed.at[other],
            dst_ref=arrived.at[lane, chip],
            send_sem=send_sem.at[d],
            recv_sem=recv_sem.at[chip],
            device_id={"side": other * members + lane},
            device_id_type=MESH,
        )
        copy.start()
        sends.append(copy)
    arrived[lane, chip] = packed[chip]

    def forward(d, source):
        for j, mate in enumerate(mates):
            copy = pltpu.make_async_remote_copy(
                src_ref=arrived.at[lane, source],
                dst_ref=arrived.at[lane, source],
                send_sem=fsend_sem.at[j, d],
                recv_sem=frecv_sem.at[lane, source],
                device_id={"side": chip * members + mate},
                device_id_type=MESH,
            )
            copy.start()
            sends.append(copy)

    forward(0, chip)

    logits = lax.dot_general(
        normed.astype(BF16), router_ref[...], (((1,), (1,)), ((), ())), preferred_element_type=F32
    )
    gap = jnp.sum((first_hot - second_hot) * logits, axis=1, keepdims=True)
    gates = first_hot * jax.nn.sigmoid(gap) + second_hot * jax.nn.sigmoid(-gap)
    combine = (
        jnp.where(cut_mask, jnp.concatenate([dot(gates.astype(BF16), spread)] * cuts, axis=0), 0.0)
        * select
    ).astype(BF16)

    r, q = iota((rows, rows), 0), iota((rows, rows), 1)
    order = (
        lax.rem(r, each) // cap * TILE + r // each * cap + lax.rem(r, cap) == q
    ).astype(BF16)

    def sources():
        return [(d, lax.rem(chip + experts - d, experts)) for d in range(1, experts)]

    for d, source in sources():
        pltpu.make_async_remote_copy(
            src_ref=packed.at[source],
            dst_ref=arrived.at[lane, source],
            send_sem=send_sem.at[d - 1],
            recv_sem=recv_sem.at[source],
            device_id={"side": source * members + lane},
            device_id_type=MESH,
        ).wait_recv()
        forward(d, source)
    for load in loads[2:]:
        load.wait()
    for d, source in [(0, chip)] + sources():
        for j, mate in enumerate(mates):
            pltpu.make_async_remote_copy(
                src_ref=arrived.at[mate, source],
                dst_ref=arrived.at[mate, source],
                send_sem=fsend_sem.at[j, d],
                recv_sem=frecv_sem.at[mate, source],
                device_id={"side": chip * members + mate},
                device_id_type=MESH,
            ).wait_recv()

    def give(b):
        for j, mate in enumerate(mates):
            copy = pltpu.make_async_remote_copy(
                src_ref=part_out.at[mate, b],
                dst_ref=part_in.at[lane, b],
                send_sem=psend_sem.at[j, b],
                recv_sem=precv_sem.at[lane, b],
                device_id={"side": chip * members + mate},
                device_id_type=MESH,
            )
            copy.start()
            sends.append(copy)

    pair = min(2, members)
    blocks = members // pair

    def expand(block):
        tokens = [
            dot(order, arrived[block * pair + n].reshape(rows, piece)).astype(BF16)
            for n in range(pair)
        ]
        gate_part = up_part = 0.0
        for b in range(cuts):
            x = jnp.concatenate([t[b * each : (b + 1) * each] for t in tokens], axis=0)
            gate_part = gate_part + dot(x, w_gate[b * piece : (b + 1) * piece, :])
            up_part = up_part + dot(x, w_up[b * piece : (b + 1) * piece, :])
        hidden[block] = (jax.nn.silu(gate_part) * up_part).astype(BF16)

    def contract(block, b):
        y = dot(hidden[block], w_down[:, b * piece : (b + 1) * piece]).reshape(pair, each, piece)
        for n in range(pair):
            partial[block * pair + n, b] = y[n]
            part_out[block * pair + n, b] = y[n].astype(BF16)

    def over(fn):
        if blocks == 1:
            fn(0)
        else:
            pl.loop(0, blocks)(fn)

    over(expand)
    for b in range(cuts):
        over(functools.partial(contract, b=b))
        give(b)

    sums = []
    for b in range(cuts):
        total = partial[lane, b]
        for j, mate in enumerate(mates):
            pltpu.make_async_remote_copy(
                src_ref=part_out.at[mate, b],
                dst_ref=part_in.at[mate, b],
                send_sem=psend_sem.at[j, b],
                recv_sem=precv_sem.at[mate, b],
                device_id={"side": chip * members + mate},
                device_id_type=MESH,
            ).wait_recv()
            total = total + part_in[mate, b].astype(F32)
        sums.append(total.astype(BF16))
    order_back = (
        lax.rem(q, each) // cap * TILE + q // each * cap + lax.rem(q, cap) == r
    ).astype(BF16)
    back_out[...] = (
        dot(order_back, jnp.concatenate(sums, axis=0)).astype(BF16).reshape(experts, TILE, piece)
    )
    for d, other in enumerate(others):
        copy = pltpu.make_async_remote_copy(
            src_ref=back_out.at[other],
            dst_ref=back_in.at[chip],
            send_sem=rsend_sem.at[d],
            recv_sem=rrecv_sem.at[chip],
            device_id={"side": other * members + lane},
            device_id_type=MESH,
        )
        copy.start()
        sends.append(copy)
    back_in[chip] = back_out[chip]
    for d, source in sources():
        pltpu.make_async_remote_copy(
            src_ref=back_out.at[source],
            dst_ref=back_in.at[source],
            send_sem=rsend_sem.at[d - 1],
            recv_sem=rrecv_sem.at[source],
            device_id={"side": source * members + lane},
            device_id_type=MESH,
        ).wait_recv()
    moe = dot(combine, back_in[...].reshape(rows, piece))
    for b in range(cuts):
        columns = slice(b * piece, (b + 1) * piece)
        out_ref[:, columns] = (mid[:, columns] + moe[b * seqs : (b + 1) * seqs]).astype(BF16)
    for copy in sends:
        copy.wait_send()


def on_device(
    query,
    new_key,
    new_value,
    key_cache,
    value_cache,
    lengths,
    residual,
    norm_gain,
    router,
    routes,
    w_gate,
    w_up,
    w_down,
):
    seqs, width = residual.shape
    experts = router.shape[1]
    side = lax.axis_size("side")
    members = side // experts
    cap = seqs // 2
    cuts = TILE // cap
    piece = width // cuts
    each = experts * cap
    pair = min(2, members)
    heads = width // HD
    vmem = pl.BlockSpec(memory_space=pltpu.VMEM)
    hbm = pl.BlockSpec(memory_space=pl.ANY)
    dma = pltpu.SemaphoreType.DMA
    return pl.pallas_call(
        functools.partial(kernel, side),
        out_shape=jax.ShapeDtypeStruct((seqs, width), BF16),
        in_specs=[vmem, vmem, vmem, pl.BlockSpec(memory_space=pltpu.SMEM)] + [vmem] * 4 + [hbm] * 5,
        out_specs=vmem,
        scratch_shapes=[
            pltpu.VMEM(key_cache.shape, BF16),
            pltpu.VMEM(value_cache.shape, BF16),
            pltpu.VMEM(w_gate.shape, BF16),
            pltpu.VMEM(w_up.shape, BF16),
            pltpu.VMEM(w_down.shape, BF16),
            pltpu.VMEM((seqs * heads, HD), F32),
            pltpu.VMEM((seqs * heads, HD), F32),
            pltpu.VMEM((experts, TILE, piece), BF16),
            pltpu.VMEM((members, experts, TILE, piece), BF16),
            pltpu.VMEM((members // pair, pair * each, w_gate.shape[1]), BF16),
            pltpu.VMEM((members, cuts, each, piece), F32),
            pltpu.VMEM((members, cuts, each, piece), BF16),
            pltpu.VMEM((members, cuts, each, piece), BF16),
            pltpu.VMEM((experts, TILE, piece), BF16),
            pltpu.VMEM((experts, TILE, piece), BF16),
            dma((5,)),
            dma((experts - 1,)),
            dma((experts,)),
            dma((members, experts)),
            dma((members, experts)),
            dma((members, cuts)),
            dma((members, cuts)),
            dma((experts - 1,)),
            dma((experts,)),
        ],
        compiler_params=pltpu.CompilerParams(
            collective_id=0, has_side_effects=True, vmem_limit_bytes=50 * 1024 * 1024
        ),
    )(
        query,
        new_key,
        new_value,
        lengths,
        residual,
        norm_gain[None, :],
        router.T,
        routes,
        key_cache,
        value_cache,
        w_gate,
        w_up,
        w_down,
    )


def solution(mesh):
    in_specs = (
        P(("groups", "side"), None),
        P(("groups", "side"), None),
        P(("groups", "side"), None),
        P(("groups", "side"), None, None),
        P(("groups", "side"), None, None),
        P(("groups", "side")),
        P(("groups", "side"), None),
        P(),
        P(),
        P(("groups", "side"), None),
        P(None, "side"),
        P(None, "side"),
        P("side", None),
    )
    out_specs = P(("groups", "side"), None)
    return jax.shard_map(
        on_device, mesh=mesh, in_specs=in_specs, out_specs=out_specs, check_vma=False
    )
```

time: 88 us -> 32.4 us (0.37); the launches traced: 86.5 us -> 31.9 us
  matrix products: 24.2 us -> 0 us
  Pallas kernels: 0 us -> 22.9 us
  starting transfers between devices: 20.7 us -> 0 us
  waiting for transfers between devices: 13.4 us -> 0 us
  local copies, waits for them, and re-layouts: 20.7 us -> 8.96 us
  other arithmetic: 7.32 us -> 0 us
    dot_general x18 -> x0, matrix products: 24.2 us -> none  [the longest x2 6.3 us: expert_rows(): gate_part = jnp.dot(tok_rows, w_gate, preferred_element_type=jnp.float32)]
    pallas_call x0 -> x1, Pallas kernels: none -> 22.9 us  [on_device(): pl.pallas_call(functools.partial(kernel, side), out_shape=jax.ShapeDtypeS...]
    all_to_all x4 -> x0, starting transfers between devices: 20.7 us -> none  [the longest x2 11.6 us: on_device(): lax.all_to_all(outgoing, 'side', split_axis=0, concat_axis=0, tiled=True)]
    all_to_all x4 -> x0, waiting for transfers between devices: 13.4 us -> none  [the longest x2 6.83 us: on_device(): lax.all_to_all(partial_value.reshape(sources, items, width).astype(jnp.bf...]
    slice x6 -> x0, local copies, waits for them, and re-layouts: 7.93 us -> none  [the longest x1 2.26 us: on_device(): key_cache[lower:upper]]
    reduce_sum x7 -> x0, other arithmetic: 2.34 us -> none  [the longest x2 1.46 us: on_device(): jnp.sum(returned.reshape(experts_all, group_size, capacity, width), axis=1)]
    convert_element_type x7 -> x0, other arithmetic: 2.22 us -> none  [the longest x1 0.78 us: attend(): own_value.astype(jnp.float32)[:, :, None, :]]
    convert_element_type x6 -> x0, local copies, waits for them, and re-layouts: 1.76 us -> none  [the longest x2 1.51 us: on_device(): partial_value.reshape(sources, items, width).astype(jnp.bfloat16)]
  transfers between devices with their start and end apart: 4 -> 0, of which waited for: 4 -> 0; matrix products, arithmetic and copies ran while one was open for 26% -> 0% of each run, Pallas kernels for 0% -> 0%
where the time goes in v1:
time: 32.4 us; the launch traced here: 31.9 us
  Pallas kernels  22.9 us (71%)
  local copies, waits for them, and re-layouts  8.96 us (28%)
    pallas_call x1, Pallas kernels, on_device(): pl.pallas_call(functools.partial(kernel, side), out_shape=jax.ShapeDtypeS...  22.9 us
    unnamed x18, local copies, waits for them, and re-layouts  8.26 us
    broadcast_in_dim x1, local copies, waits for them, and re-layouts, on_device(): norm_gain[None, :]  0.7 us

profile of v1, /device:TPU:0, one launch (start us, length us, event | category | flops | bytes accessed | tf_op | source)
XLA Modules:
  0.0 31.9 jit_solution(14930652661400251528)
XLA Ops:
  0.0 0.8 %copy.14.routes_ref = s32[8,2]{1,0:T(8,128)S(1)} copy(s32[8,2]{0,1:T(2,128)} %param.22) | data formatting | bytes 128 | tf_op args[9]
  0.8 0.7 %broadcast_in_dim.3.gain_ref = bf16[1,3072]{1,0:T(2,128)(2,1)S(1)} reshape(bf16[3072]{0:T(1024)(128)(2,1)} %param.20) | data formatting | bytes 12288 | tf_op jit(solution)/shard_map/broadcast_in_dim | solution.py:409
  1.5 0.0 copy-start
  1.5 1.2 %copy-done = bf16[8,128,512]{2,1,0:T(8,128)(2,1)S(1)} copy-done((bf16[8,128,512]{2,1,0:T(8,128)(2,1)S(1)}, bf16[8,128,512]{2,1,0:T(8,128)(2,1)}, u32[]{:S(2)}) %copy-start) | copy-done | bytes 1048600
  2.7 0.0 copy-start.1
  2.7 1.2 %copy-done.1 = bf16[8,128,512]{2,1,0:T(8,128)(2,1)S(1)} copy-done((bf16[8,128,512]{2,1,0:T(8,128)(2,1)S(1)}, bf16[8,128,512]{2,1,0:T(8,128)(2,1)}, u32[]{:S(2)}) %copy-start.1) | copy-done | bytes 1048600
  3.9 0.0 copy-start.2
  3.9 0.8 %copy-done.2 = bf16[8,3072]{1,0:T(8,128)(2,1)S(1)} copy-done((bf16[8,3072]{1,0:T(8,128)(2,1)S(1)}, bf16[8,3072]{1,0:T(8,128)(2,1)}, u32[]{:S(2)}) %copy-start.2) | copy-done | bytes 49176
  4.7 0.0 copy-start.3
  4.7 0.8 %copy-done.3 = bf16[8,3072]{1,0:T(8,128)(2,1)S(1)} copy-done((bf16[8,3072]{1,0:T(8,128)(2,1)S(1)}, bf16[8,3072]{1,0:T(8,128)(2,1)}, u32[]{:S(2)}) %copy-start.3) | copy-done | bytes 49176
  5.5 0.0 copy-start.4
  5.5 0.8 %copy-done.4 = bf16[3072,8]{0,1:T(8,128)(2,1)S(1)} copy-done((bf16[3072,8]{0,1:T(8,128)(2,1)S(1)}, bf16[3072,8]{0,1:T(8,128)(2,1)}, u32[]{:S(2)}) %copy-start.4) | copy-done | bytes 49176
  6.3 0.0 copy-start.5
  6.3 0.7 %copy-done.5 = bf16[8,512]{1,0:T(8,128)(2,1)S(1)} copy-done((bf16[8,512]{1,0:T(8,128)(2,1)S(1)}, bf16[8,512]{1,0:T(8,128)(2,1)}, u32[]{:S(2)}) %copy-start.5) | copy-done | bytes 8216
  7.0 0.0 copy-start.6
  7.0 0.7 %copy-done.6 = bf16[8,512]{1,0:T(8,128)(2,1)S(1)} copy-done((bf16[8,512]{1,0:T(8,128)(2,1)S(1)}, bf16[8,512]{1,0:T(8,128)(2,1)}, u32[]{:S(2)}) %copy-start.6) | copy-done | bytes 8216
  7.7 0.0 copy-start.7
  7.7 0.7 %copy-done.7 = s32[8]{0:T(128)S(1)} copy-done((s32[8]{0:T(128)S(1)}, s32[8]{0:T(128)}, u32[]{:S(2)}) %copy-start.7) | copy-done | bytes 56
  8.4 22.9 %shard_map.127 = bf16[8,3072]{1,0:T(8,128)(2,1)S(1)} custom-call(bf16[8,3072]{1,0:T(8,128)(2,1)S(1)} %copy-done.2, bf16[8,512]{1,0:T(8,128)(2,1)S(1)} %copy-done.5, bf16[8,512]{1,0:T(8,128)(2,1)S(1)} %copy-done.6, s32[8]{0:T(128)S(1)} %copy-done.7, bf16[8,3072]{1,0:T(8,128)(2,1)S(1)} %copy-done.3, bf16[1,3072]{1,0:T(2,128)(2,1)S(1)} %broadcast_in_dim.3.gain_ref, ...), custom_call_target="tpu_custom_call" | custom-call | tf_op jit(solution)/shard_map/pallas_call | solution.py:369
  31.3 0.6 %copy.16 = bf16[8,3072]{1,0:T(8,128)(2,1)} copy(bf16[8,3072]{1,0:T(8,128)(2,1)S(1)} %shard_map.127) | data formatting | bytes 98304
Async XLA Ops:
  1.5 1.2 %copy-start = (bf16[8,128,512]{2,1,0:T(8,128)(2,1)S(1)}, bf16[8,128,512]{2,1,0:T(8,128)(2,1)}, u32[]{:S(2)}) copy-start(bf16[8,128,512]{2,1,0:T(8,128)(2,1)} %key_hbm.1) | copy-start | bytes 3145732
  2.7 1.2 %copy-start.1 = (bf16[8,128,512]{2,1,0:T(8,128)(2,1)S(1)}, bf16[8,128,512]{2,1,0:T(8,128)(2,1)}, u32[]{:S(2)}) copy-start(bf16[8,128,512]{2,1,0:T(8,128)(2,1)} %value_hbm.1) | copy-start | bytes 3145732
  3.9 0.8 %copy-start.2 = (bf16[8,3072]{1,0:T(8,128)(2,1)S(1)}, bf16[8,3072]{1,0:T(8,128)(2,1)}, u32[]{:S(2)}) copy-start(bf16[8,3072]{1,0:T(8,128)(2,1)} %query_ref.1) | copy-start | bytes 147460
  4.7 0.8 %copy-start.3 = (bf16[8,3072]{1,0:T(8,128)(2,1)S(1)}, bf16[8,3072]{1,0:T(8,128)(2,1)}, u32[]{:S(2)}) copy-start(bf16[8,3072]{1,0:T(8,128)(2,1)} %residual_ref.1) | copy-start | bytes 147460
  5.5 0.8 %copy-start.4 = (bf16[3072,8]{0,1:T(8,128)(2,1)S(1)}, bf16[3072,8]{0,1:T(8,128)(2,1)}, u32[]{:S(2)}) copy-start(bf16[3072,8]{0,1:T(8,128)(2,1)} %param.21) | copy-start | bytes 147460
  6.3 0.7 %copy-start.5 = (bf16[8,512]{1,0:T(8,128)(2,1)S(1)}, bf16[8,512]{1,0:T(8,128)(2,1)}, u32[]{:S(2)}) copy-start(bf16[8,512]{1,0:T(8,128)(2,1)} %new_key_ref.1) | copy-start | bytes 24580
  7.0 0.7 %copy-start.6 = (bf16[8,512]{1,0:T(8,128)(2,1)S(1)}, bf16[8,512]{1,0:T(8,128)(2,1)}, u32[]{:S(2)}) copy-start(bf16[8,512]{1,0:T(8,128)(2,1)} %new_value_ref.1) | copy-start | bytes 24580
  7.7 0.7 %copy-start.7 = (s32[8]{0:T(128)S(1)}, s32[8]{0:T(128)}, u32[]{:S(2)}) copy-start(s32[8]{0:T(128)} %lengths_ref.1) | copy-start | bytes 100

commit v2 on v1

--- a/solution.py
+++ b/solution.py
@@ -33,7 +33,6 @@
     for h in range(heads):
         q_rows[pl.ds(h, seqs, stride=heads), :] = query[:, h * HD : (h + 1) * HD]
     own_keys = new_key_ref[...].astype(F32)
-    own_values = new_value_ref[...].astype(F32)
     mine = iota((heads, kv), 0) // group == iota((heads, kv), 1) // HD
     position = iota((heads, slots), 1)
     scores, own = [], []
@@ -46,6 +45,7 @@
         scores.append(jnp.where(position < lengths_ref[s], score * scale, -jnp.inf))
         own.append(jnp.sum(wide * own_keys[s : s + 1, :], axis=1, keepdims=True) * scale)
     values_ready()
+    own_values = new_value_ref[...].astype(F32)
     for s in range(seqs):
         top = jnp.maximum(jnp.max(scores[s], axis=1, keepdims=True), own[s])
         weights = jnp.exp(scores[s] - top)
@@ -65,6 +65,20 @@
 
 def kernel(
     side,
+    query_hbm,
+    new_key_hbm,
+    new_value_hbm,
+    lengths_hbm,
+    residual_hbm,
+    gain_hbm,
+    router_hbm,
+    routes_hbm,
+    key_hbm,
+    value_hbm,
+    gate_hbm,
+    up_hbm,
+    down_hbm,
+    out_ref,
     query_ref,
     new_key_ref,
     new_value_ref,
@@ -73,12 +87,6 @@
     gain_ref,
     router_ref,
     routes_ref,
-    key_hbm,
-    value_hbm,
-    gate_hbm,
-    up_hbm,
-    down_hbm,
-    out_ref,
     keys,
     values,
     w_gate,
@@ -104,8 +112,8 @@
     rsend_sem,
     rrecv_sem,
 ):
-    seqs, width = residual_ref.shape
-    experts = router_ref.shape[0]
+    seqs, width = residual_hbm.shape
+    experts = router_hbm.shape[0]
     members = side // experts
     cap = seqs // 2
     cuts = TILE // cap
@@ -119,8 +127,16 @@
     loads = []
     for n, (src, dst) in enumerate(
         (
+            (routes_hbm, routes_ref),
+            (query_hbm, query_ref),
+            (lengths_hbm, lengths_ref),
+            (new_key_hbm, new_key_ref),
             (key_hbm, keys),
+            (new_value_hbm, new_value_ref),
             (value_hbm, values),
+            (residual_hbm, residual_ref),
+            (gain_hbm, gain_ref),
+            (router_hbm, router_ref),
             (gate_hbm, w_gate),
             (up_hbm, w_up),
             (down_hbm, w_down),
@@ -143,8 +159,14 @@
         )
 
     ids = iota((seqs, experts), 1)
-    first_hot = (routes_ref[:, 0:1] == ids).astype(F32)
-    second_hot = (routes_ref[:, 1:2] == ids).astype(F32)
+    loads[0].wait()
+    diagonal = iota((seqs, seqs), 0) == iota((seqs, seqs), 1)
+    first_hot, second_hot = [
+        (
+            jnp.sum(jnp.where(diagonal, routes_ref[n : n + 1, :], 0), axis=1, keepdims=True) == ids
+        ).astype(F32)
+        for n in range(2)
+    ]
     routed = (first_hot + second_hot).astype(BF16)
     earlier = (iota((seqs, seqs), 0) > iota((seqs, seqs), 1)).astype(BF16)
     rank = dot(earlier, routed).astype(BF16)
@@ -156,15 +178,21 @@
     )
     select = jnp.where(cut_mask, jnp.concatenate([chosen] * cuts, axis=0), 0.0)
 
-    loads[0].wait()
+    for load in loads[1:5]:
+        load.wait()
+
+    def values_ready():
+        for load in loads[5:10]:
+            load.wait()
+
     attention = attend(
-        query_ref, new_key_ref, new_value_ref, lengths_ref, keys, values, loads[1].wait, q_rows, o_rows
+        query_ref, new_key_ref, new_value_ref, lengths_ref, keys, values, values_ready, q_rows, o_rows
     )
     mid = (residual_ref[...].astype(F32) + attention).astype(BF16).astype(F32)
     normed = (
         mid
         * lax.rsqrt(jnp.mean(mid * mid, axis=1, keepdims=True) + 1e-05)
-        * gain_ref[...].astype(F32)
+        * gain_ref[...].astype(F32).reshape(1, width)
     )
     stacked = jnp.concatenate(
         [normed[:, b * piece : (b + 1) * piece] for b in range(cuts)], axis=0
@@ -231,7 +259,7 @@
             device_id_type=MESH,
         ).wait_recv()
         forward(d, source)
-    for load in loads[2:]:
+    for load in loads[10:]:
         load.wait()
     for d, source in [(0, chip)] + sources():
         for j, mate in enumerate(mates):
@@ -364,14 +392,22 @@
     pair = min(2, members)
     heads = width // HD
     vmem = pl.BlockSpec(memory_space=pltpu.VMEM)
-    hbm = pl.BlockSpec(memory_space=pl.ANY)
+    hbm = pl.BlockSpec(memory_space=pltpu.HBM)
     dma = pltpu.SemaphoreType.DMA
     return pl.pallas_call(
         functools.partial(kernel, side),
         out_shape=jax.ShapeDtypeStruct((seqs, width), BF16),
-        in_specs=[vmem, vmem, vmem, pl.BlockSpec(memory_space=pltpu.SMEM)] + [vmem] * 4 + [hbm] * 5,
+        in_specs=[hbm] * 13,
         out_specs=vmem,
         scratch_shapes=[
+            pltpu.VMEM(query.shape, BF16),
+            pltpu.VMEM(new_key.shape, BF16),
+            pltpu.VMEM(new_value.shape, BF16),
+            pltpu.SMEM(lengths.shape, jnp.int32),
+            pltpu.VMEM(residual.shape, BF16),
+            pltpu.VMEM(norm_gain.shape, BF16),
+            pltpu.VMEM((experts, width), BF16),
+            pltpu.VMEM((2, seqs), jnp.int32),
             pltpu.VMEM(key_cache.shape, BF16),
             pltpu.VMEM(value_cache.shape, BF16),
             pltpu.VMEM(w_gate.shape, BF16),
@@ -387,7 +423,7 @@
             pltpu.VMEM((members, cuts, each, piece), BF16),
             pltpu.VMEM((experts, TILE, piece), BF16),
             pltpu.VMEM((experts, TILE, piece), BF16),
-            dma((5,)),
+            dma((13,)),
             dma((experts - 1,)),
             dma((experts,)),
             dma((members, experts)),
@@ -398,7 +434,7 @@
             dma((experts,)),
         ],
         compiler_params=pltpu.CompilerParams(
-            collective_id=0, has_side_effects=True, vmem_limit_bytes=50 * 1024 * 1024
+            collective_id=0, has_side_effects=True, vmem_limit_bytes=64 * 1024 * 1024
         ),
     )(
         query,
@@ -406,9 +442,9 @@
         new_value,
         lengths,
         residual,
-        norm_gain[None, :],
+        norm_gain,
         router.T,
-        routes,
+        routes.T,
         key_cache,
         value_cache,
         w_gate,

time: 32.4 us -> 24.5 us (0.76); the launches traced: 31.9 us -> 24.4 us
  local copies, waits for them, and re-layouts: 8.96 us -> 1.42 us
    unnamed x18 -> x1, local copies, waits for them, and re-layouts: 8.26 us -> 1.42 us
    broadcast_in_dim x1 -> x0, local copies, waits for them, and re-layouts: 0.7 us -> none  [on_device(): norm_gain[None, :]]
where the time goes in v2:
time: 24.5 us; the launch traced here: 24.4 us
  Pallas kernels  22.9 us (93%)
  local copies, waits for them, and re-layouts  1.42 us (6%)
    pallas_call x1, Pallas kernels, on_device(): pl.pallas_call(functools.partial(kernel, side), out_shape=jax.ShapeDtypeS...  22.9 us
    unnamed x1, local copies, waits for them, and re-layouts  1.42 us

profile of v2, /device:TPU:0, one launch (start us, length us, event | category | flops | bytes accessed | tf_op | source)
XLA Modules:
  0.0 24.4 jit_solution(13173439811074431302)
XLA Ops:
  0.0 22.9 %shard_map.127 = bf16[8,3072]{1,0:T(8,128)(2,1)} custom-call(bf16[8,3072]{1,0:T(8,128)(2,1)} %query_hbm.1, bf16[8,512]{1,0:T(8,128)(2,1)} %new_key_hbm.1, bf16[8,512]{1,0:T(8,128)(2,1)} %new_value_hbm.1, s32[8]{0:T(128)} %lengths_hbm.1, bf16[8,3072]{1,0:T(8,128)(2,1)} %residual_hbm.1, bf16[3072]{0:T(1024)(128)(2,1)} %gain_hbm.1, bf16[8,3072]{1,0:T(8,128)(2,1)} %bitcast.2, ...), custom_call_target="tpu_custom_call" | custom-call | tf_op jit(solution)/shard_map/pallas_call | solution.py:397
  23.0 1.4 %copy.15 = bf16[8,3072]{1,0:T(8,128)(2,1)} copy(bf16[8,3072]{1,0:T(8,128)(2,1)} %shard_map.127) | data formatting | bytes 98304

commit v3 on v2

--- a/solution.py
+++ b/solution.py
@@ -9,6 +9,7 @@
 
 HD = 128
 TILE = 16
+PART = 256
 F32 = jnp.float32
 BF16 = jnp.bfloat16
 MESH = pl.DeviceIdType.MESH
@@ -143,7 +144,8 @@
         )
     ):
         load = pltpu.make_async_copy(src, dst, load_sem.at[n])
-        load.start()
+        if n < 10:
+            load.start()
         loads.append(load)
 
     others = [lax.rem(chip + d, experts) for d in range(1, experts)]
@@ -180,6 +182,8 @@
 
     for load in loads[1:5]:
         load.wait()
+    for load in loads[10:]:
+        load.start()
 
     def values_ready():
         for load in loads[5:10]:
@@ -272,13 +276,16 @@
                 device_id_type=MESH,
             ).wait_recv()
 
-    def give(b):
+    parts = partial.shape[1]
+    wide = piece // parts
+
+    def give(p):
         for j, mate in enumerate(mates):
             copy = pltpu.make_async_remote_copy(
-                src_ref=part_out.at[mate, b],
-                dst_ref=part_in.at[lane, b],
-                send_sem=psend_sem.at[j, b],
-                recv_sem=precv_sem.at[lane, b],
+                src_ref=part_out.at[mate, p],
+                dst_ref=part_in.at[lane, p],
+                send_sem=psend_sem.at[j, p],
+                recv_sem=precv_sem.at[lane, p],
                 device_id={"side": chip * members + mate},
                 device_id_type=MESH,
             )
@@ -300,11 +307,13 @@
             up_part = up_part + dot(x, w_up[b * piece : (b + 1) * piece, :])
         hidden[block] = (jax.nn.silu(gate_part) * up_part).astype(BF16)
 
-    def contract(block, b):
-        y = dot(hidden[block], w_down[:, b * piece : (b + 1) * piece]).reshape(pair, each, piece)
-        for n in range(pair):
-            partial[block * pair + n, b] = y[n]
-            part_out[block * pair + n, b] = y[n].astype(BF16)
+    def contract(block, p):
+        for b in range(cuts):
+            start = b * piece + p * wide
+            y = dot(hidden[block], w_down[:, start : start + wide]).reshape(pair, each, wide)
+            for n in range(pair):
+                partial[block * pair + n, p, b * each : (b + 1) * each, :] = y[n]
+                part_out[block * pair + n, p, b * each : (b + 1) * each, :] = y[n].astype(BF16)
 
     def over(fn):
         if blocks == 1:
@@ -312,56 +321,58 @@
         else:
             pl.loop(0, blocks)(fn)
 
-    over(expand)
-    for b in range(cuts):
-        over(functools.partial(contract, b=b))
-        give(b)
-
-    sums = []
-    for b in range(cuts):
-        total = partial[lane, b]
-        for j, mate in enumerate(mates):
-            pltpu.make_async_remote_copy(
-                src_ref=part_out.at[mate, b],
-                dst_ref=part_in.at[mate, b],
-                send_sem=psend_sem.at[j, b],
-                recv_sem=precv_sem.at[mate, b],
-                device_id={"side": chip * members + mate},
-                device_id_type=MESH,
-            ).wait_recv()
-            total = total + part_in[mate, b].astype(F32)
-        sums.append(total.astype(BF16))
     order_back = (
         lax.rem(q, each) // cap * TILE + q // each * cap + lax.rem(q, cap) == r
     ).astype(BF16)
-    back_out[...] = (
-        dot(order_back, jnp.concatenate(sums, axis=0)).astype(BF16).reshape(experts, TILE, piece)
-    )
-    for d, other in enumerate(others):
-        copy = pltpu.make_async_remote_copy(
-            src_ref=back_out.at[other],
-            dst_ref=back_in.at[chip],
-            send_sem=rsend_sem.at[d],
-            recv_sem=rrecv_sem.at[chip],
-            device_id={"side": other * members + lane},
-            device_id_type=MESH,
-        )
-        copy.start()
-        sends.append(copy)
-    back_in[chip] = back_out[chip]
-    for d, source in sources():
-        pltpu.make_async_remote_copy(
-            src_ref=back_out.at[source],
-            dst_ref=back_in.at[source],
-            send_sem=rsend_sem.at[d - 1],
-            recv_sem=rrecv_sem.at[source],
-            device_id={"side": source * members + lane},
-            device_id_type=MESH,
-        ).wait_recv()
-    moe = dot(combine, back_in[...].reshape(rows, piece))
-    for b in range(cuts):
-        columns = slice(b * piece, (b + 1) * piece)
-        out_ref[:, columns] = (mid[:, columns] + moe[b * seqs : (b + 1) * seqs]).astype(BF16)
+
+    def collect(p):
+        total = partial[lane, p]
+        for j, mate in enumerate(mates):
+            pltpu.make_async_remote_copy(
+                src_ref=part_out.at[mate, p],
+                dst_ref=part_in.at[mate, p],
+                send_sem=psend_sem.at[j, p],
+                recv_sem=precv_sem.at[mate, p],
+                device_id={"side": chip * members + mate},
+                device_id_type=MESH,
+            ).wait_recv()
+            total = total + part_in[mate, p].astype(F32)
+        back_out[p] = dot(order_back, total.astype(BF16)).astype(BF16).reshape(experts, TILE, wide)
+        for d, other in enumerate(others):
+            copy = pltpu.make_async_remote_copy(
+                src_ref=back_out.at[p, other],
+                dst_ref=back_in.at[p, chip],
+                send_sem=rsend_sem.at[p, d],
+                recv_sem=rrecv_sem.at[p, chip],
+                device_id={"side": other * members + lane},
+                device_id_type=MESH,
+            )
+            copy.start()
+            sends.append(copy)
+        back_in[p, chip] = back_out[p, chip]
+
+    over(expand)
+    for p in range(parts):
+        over(functools.partial(contract, p=p))
+        give(p)
+        if p > 0:
+            collect(p - 1)
+    collect(parts - 1)
+
+    for p in range(parts):
+        for d, source in sources():
+            pltpu.make_async_remote_copy(
+                src_ref=back_out.at[p, source],
+                dst_ref=back_in.at[p, source],
+                send_sem=rsend_sem.at[p, d - 1],
+                recv_sem=rrecv_sem.at[p, source],
+                device_id={"side": source * members + lane},
+                device_id_type=MESH,
+            ).wait_recv()
+        moe = dot(combine, back_in[p].reshape(rows, wide))
+        for b in range(cuts):
+            columns = slice(b * piece + p * wide, b * piece + (p + 1) * wide)
+            out_ref[:, columns] = (mid[:, columns] + moe[b * seqs : (b + 1) * seqs]).astype(BF16)
     for copy in sends:
         copy.wait_send()
 
@@ -389,6 +400,9 @@
     cuts = TILE // cap
     piece = width // cuts
     each = experts * cap
+    rows = experts * TILE
+    parts = piece // PART
+    wide = piece // parts
     pair = min(2, members)
     heads = width // HD
     vmem = pl.BlockSpec(memory_space=pltpu.VMEM)
@@ -418,20 +432,20 @@
             pltpu.VMEM((experts, TILE, piece), BF16),
             pltpu.VMEM((members, experts, TILE, piece), BF16),
             pltpu.VMEM((members // pair, pair * each, w_gate.shape[1]), BF16),
-            pltpu.VMEM((members, cuts, each, piece), F32),
-            pltpu.VMEM((members, cuts, each, piece), BF16),
-            pltpu.VMEM((members, cuts, each, piece), BF16),
-            pltpu.VMEM((experts, TILE, piece), BF16),
-            pltpu.VMEM((experts, TILE, piece), BF16),
+            pltpu.VMEM((members, parts, rows, wide), F32),
+            pltpu.VMEM((members, parts, rows, wide), BF16),
+            pltpu.VMEM((members, parts, rows, wide), BF16),
+            pltpu.VMEM((parts, experts, TILE, wide), BF16),
+            pltpu.VMEM((parts, experts, TILE, wide), BF16),
             dma((13,)),
             dma((experts - 1,)),
             dma((experts,)),
             dma((members, experts)),
             dma((members, experts)),
-            dma((members, cuts)),
-            dma((members, cuts)),
-            dma((experts - 1,)),
-            dma((experts,)),
+            dma((members, parts)),
+            dma((members, parts)),
+            dma((parts, experts - 1)),
+            dma((parts, experts)),
         ],
         compiler_params=pltpu.CompilerParams(
             collective_id=0, has_side_effects=True, vmem_limit_bytes=64 * 1024 * 1024

time: 24.5 us -> 24.6 us (level)
  no operation moved by 1% of the time
where the time goes in v3:
time: 24.6 us; the launch traced here: 24.4 us
  Pallas kernels  23 us (93%)
  local copies, waits for them, and re-layouts  1.42 us (6%)
    pallas_call x1, Pallas kernels, on_device(): pl.pallas_call(functools.partial(kernel, side), out_shape=jax.ShapeDtypeS...  23 us
    unnamed x1, local copies, waits for them, and re-layouts  1.42 us

profile of v3, /device:TPU:0, one launch (start us, length us, event | category | flops | bytes accessed | tf_op | source)
XLA Modules:
  0.0 24.4 jit_solution(4949417661461864761)
XLA Ops:
  0.0 23.0 %shard_map.127 = bf16[8,3072]{1,0:T(8,128)(2,1)} custom-call(bf16[8,3072]{1,0:T(8,128)(2,1)} %query_hbm.1, bf16[8,512]{1,0:T(8,128)(2,1)} %new_key_hbm.1, bf16[8,512]{1,0:T(8,128)(2,1)} %new_value_hbm.1, s32[8]{0:T(128)} %lengths_hbm.1, bf16[8,3072]{1,0:T(8,128)(2,1)} %residual_hbm.1, bf16[3072]{0:T(1024)(128)(2,1)} %gain_hbm.1, bf16[8,3072]{1,0:T(8,128)(2,1)} %bitcast.2, ...), custom_call_target="tpu_custom_call" | custom-call | tf_op jit(solution)/shard_map/pallas_call | solution.py:411
  23.0 1.4 %copy.15 = bf16[8,3072]{1,0:T(8,128)(2,1)} copy(bf16[8,3072]{1,0:T(8,128)(2,1)} %shard_map.127) | data formatting | bytes 98304

commit v4 on v3

--- a/solution.py
+++ b/solution.py
@@ -410,7 +410,7 @@
     dma = pltpu.SemaphoreType.DMA
     return pl.pallas_call(
         functools.partial(kernel, side),
-        out_shape=jax.ShapeDtypeStruct((seqs, width), BF16),
+        out_shape=pltpu.VMEM((seqs, width), BF16),
         in_specs=[hbm] * 13,
         out_specs=vmem,
         scratch_shapes=[
@@ -448,22 +448,27 @@
             dma((parts, experts)),
         ],
         compiler_params=pltpu.CompilerParams(
-            collective_id=0, has_side_effects=True, vmem_limit_bytes=64 * 1024 * 1024
+            collective_id=0, has_side_effects=True, vmem_limit_bytes=56 * 1024 * 1024
         ),
     )(
-        query,
-        new_key,
-        new_value,
-        lengths,
-        residual,
-        norm_gain,
-        router.T,
-        routes.T,
-        key_cache,
-        value_cache,
-        w_gate,
-        w_up,
-        w_down,
+        *[
+            pltpu.with_memory_space_constraint(x, pltpu.HBM)
+            for x in (
+                query,
+                new_key,
+                new_value,
+                lengths,
+                residual,
+                norm_gain,
+                router.T,
+                routes.T,
+                key_cache,
+                value_cache,
+                w_gate,
+                w_up,
+                w_down,
+            )
+        ]
     )
 
 

time: 24.6 us -> 23.1 us (0.939)
  local copies, waits for them, and re-layouts: 1.42 us -> 0.62 us
  Pallas kernels: 23 us -> 22.4 us
    unnamed x1, local copies, waits for them, and re-layouts: 1.42 us -> 0.62 us
    pallas_call x1, Pallas kernels: 23 us -> 22.4 us  [on_device(): pl.pallas_call(functools.partial(kernel, side), out_shape=pltpu.VMEM((seq...]
where the time goes in v4:
time: 23.1 us; the launch traced here: 23 us
  Pallas kernels  22.4 us (97%)
  local copies, waits for them, and re-layouts  0.62 us (3%)
    pallas_call x1, Pallas kernels, on_device(): pl.pallas_call(functools.partial(kernel, side), out_shape=pltpu.VMEM((seq...  22.4 us
    unnamed x1, local copies, waits for them, and re-layouts  0.62 us

profile of v4, /device:TPU:0, one launch (start us, length us, event | category | flops | bytes accessed | tf_op | source)
XLA Modules:
  0.0 23.0 jit_solution(10080612725764574871)
XLA Ops:
  0.0 22.4 %shard_map.127 = bf16[8,3072]{1,0:T(8,128)(2,1)S(1)} custom-call(bf16[8,3072]{1,0:T(8,128)(2,1)} %query_hbm.1, bf16[8,512]{1,0:T(8,128)(2,1)} %new_key_hbm.1, bf16[8,512]{1,0:T(8,128)(2,1)} %new_value_hbm.1, s32[8]{0:T(128)} %lengths_hbm.1, bf16[8,3072]{1,0:T(8,128)(2,1)} %residual_hbm.1, bf16[3072]{0:T(1024)(128)(2,1)} %gain_hbm.1, ...), custom_call_target="tpu_custom_call" | custom-call | tf_op jit(solution)/shard_map/pallas_call | solution.py:411
  22.4 0.6 %copy.15 = bf16[8,3072]{1,0:T(8,128)(2,1)} copy(bf16[8,3072]{1,0:T(8,128)(2,1)S(1)} %shard_map.127) | data formatting | bytes 98304

commit v5 on v4

--- a/solution.py
+++ b/solution.py
@@ -9,7 +9,7 @@
 
 HD = 128
 TILE = 16
-PART = 256
+PART = 384
 F32 = jnp.float32
 BF16 = jnp.bfloat16
 MESH = pl.DeviceIdType.MESH

time: 23.1 us -> 23.3 us (level)
  no operation moved by 1% of the time
where the time goes in v5:
time: 23.3 us; the launch traced here: 23.1 us
  Pallas kernels  22.5 us (97%)
  local copies, waits for them, and re-layouts  0.62 us (3%)
    pallas_call x1, Pallas kernels, on_device(): pl.pallas_call(functools.partial(kernel, side), out_shape=pltpu.VMEM((seq...  22.5 us
    unnamed x1, local copies, waits for them, and re-layouts  0.62 us

profile of v5, /device:TPU:0, one launch (start us, length us, event | category | flops | bytes accessed | tf_op | source)
XLA Modules:
  0.0 23.1 jit_solution(3328804435826396414)
XLA Ops:
  0.0 22.5 %shard_map.127 = bf16[8,3072]{1,0:T(8,128)(2,1)S(1)} custom-call(bf16[8,3072]{1,0:T(8,128)(2,1)} %query_hbm.1, bf16[8,512]{1,0:T(8,128)(2,1)} %new_key_hbm.1, bf16[8,512]{1,0:T(8,128)(2,1)} %new_value_hbm.1, s32[8]{0:T(128)} %lengths_hbm.1, bf16[8,3072]{1,0:T(8,128)(2,1)} %residual_hbm.1, bf16[3072]{0:T(1024)(128)(2,1)} %gain_hbm.1, ...), custom_call_target="tpu_custom_call" | custom-call | tf_op jit(solution)/shard_map/pallas_call | solution.py:411
  22.5 0.6 %copy.15 = bf16[8,3072]{1,0:T(8,128)(2,1)} copy(bf16[8,3072]{1,0:T(8,128)(2,1)S(1)} %shard_map.127) | data formatting | bytes 98304
